TPU v7x, 512 devices: a whole 4x8x8 slice. The times are simulated.
512 devices in a mesh: dp: 16 (over z, core), tensor: 32 (over x, y).
Axes of the slice: x: 4, y: 8, z: 8, core: 2. Of those that a mesh axis runs over, the one named last changes fastest.
Arguments:
- activations: bfloat16 [12288, 4096], P('dp', 'tensor'), may hold values from -6 to 6
- out_grads_t: bfloat16 [5504, 12288], P('tensor', 'dp'), may hold values from -6 to 6
- in_basis: bfloat16 [4096, 4096], P(None, 'tensor'), may hold values from -0.09375 to 0.09375
- out_basis_t: bfloat16 [5504, 5504], P('tensor'), may hold values from -0.078125 to 0.078125
- query_proj: bfloat16 [4, 5504, 4096], P(None, 'tensor', 'dp'), may hold values from -6 to 6
- eigvals: float32 [5504, 4096], P('tensor', 'dp'), may hold values from 0.05 to 5
- damping: float32 [1], replicated, may hold values from 0.05 to 0.2
- lengths: int32 [96], P('dp'), may hold values from 1 to 128, 7680 in all
Outputs:
- scores: float32 [96, 4], P('dp')
Inputs may be any that keep to these rules, and one draw needn't show every extreme that they name: `lengths`: the largest token count is exactly 128.
All inputs are finite; a program needn't handle non-finite values. No bound on the sum of `lengths` on one device may be relied on, other than what follows from the above.
Results may differ from a plain program's by a relative error of at most 0.006.
Values may be sent and summed in bfloat16 or wider, within the bound.
No kernel may reach another device: no remote copies, remote signals or barrier semaphores. Data moves between devices by JAX's collectives and lax.ppermute only.
A program may use at most 128 MiB of HBM per device.

v0:
```python
import jax
import jax.numpy as jnp
from jax import lax
from jax.sharding import PartitionSpec as P


def local(activations, out_grads_t, in_basis, out_basis_t, query_proj, eigvals, damping, lengths):
    full_act = lax.all_gather(activations, "tensor", axis=1, tiled=True)
    act_local = jnp.dot(full_act, in_basis, preferred_element_type=jnp.float32).astype(jnp.bfloat16)
    act_proj = lax.all_gather(act_local, "tensor", axis=1, tiled=True)
    token_rows = full_act.shape[0]
    width = out_basis_t.shape[0]
    grad_full = jnp.dot(
        out_basis_t,
        lax.all_gather(out_grads_t, "tensor", axis=0, tiled=True),
        preferred_element_type=jnp.float32,
    )
    seq_count = lengths.shape[0]
    seq_len = token_rows // seq_count
    position = lax.broadcasted_iota(jnp.int32, (seq_count, seq_len), 1)
    keep = (position < lengths[:, None]).astype(jnp.float32).reshape(1, token_rows)
    grad_proj = (grad_full * keep).astype(jnp.bfloat16)
    scaled = (query_proj.astype(jnp.float32) / (eigvals + damping[0])).astype(jnp.bfloat16)
    projected = jnp.einsum(
        "jst,std->sjd",
        grad_proj.reshape(width, seq_count, seq_len),
        act_proj.reshape(seq_count, seq_len, act_proj.shape[1]),
        preferred_element_type=jnp.float32,
    )
    partial_value = jnp.einsum(
        "sij,qij->sq",
        projected,
        lax.all_gather(scaled, "dp", axis=2, tiled=True).astype(jnp.float32),
    )
    totals = lax.psum(partial_value, "tensor")
    norm_factor = (act_proj.shape[1] * out_basis_t.shape[1] * seq_len) ** (-0.5)
    return totals * norm_factor


def solution(mesh):
    placed = (
        P("dp", "tensor"),
        P("tensor", "dp"),
        P(None, "tensor"),
        P("tensor", None),
        P(None, "tensor", "dp"),
        P("tensor", "dp"),
        P(),
        P("dp"),
    )
    return jax.shard_map(
        local, mesh=mesh, in_specs=placed, out_specs=P("dp", None), check_vma=False
    )
```

profile of v0, /device:TPU:64, one launch (start us, length us, event | category | flops | bytes accessed | tf_op | source)
XLA Modules:
  0.0 474.7 jit_solution(10755105774203012612)
XLA Ops:
  6.5 0.0 copy-start
  6.5 0.0 all-gather.6.cloned.1.call-start
  6.6 0.7 all-gather.6.cloned.1.call-update
  7.3 0.0 all-gather.12.cloned.1.call-start
  7.3 0.7 all-gather.12.cloned.1.call-update
  8.0 0.0 all-gather.8.cloned.1.call-start
  8.1 104.2 %all-gather.6.cloned.1.call-done = bf16[768,4096]{1,0:T(8,128)(2,1)} async-done(((bf16[768,128]{1,0:T(8,128)(2,1)}), bf16[768,4096]{1,0:T(8,128)(2,1)}) %all-gather.6.cloned.1.call-update) | async-done | bytes 6291472 | tf_op jit(solution)/shard_map/all_gather | solution.py:8
  112.3 5.5 %convolution_convert_fusion = bf16[768,128]{1,0:T(8,128)(2,1)} fusion(bf16[768,4096]{1,0:T(8,128)(2,1)} %all-gather.6.cloned.1.call-done, bf16[4096,128]{1,0:T(8,128)(2,1)} %param.10), kind=kOutput, calls=%fused_computation.4 | convolution fusion | flops 805404672 | bytes 7536640 | tf_op jit(solution)/shard_map/dot_general | solution.py:9
  117.8 0.0 all-gather.8.cloned.1.call-update
  117.8 0.0 all-gather.10.cloned.1.call-start
  118.5 0.0 copy-done.2
  118.5 0.9 fusion.6
  119.5 0.0 all-gather.10.cloned.1.call-update
  119.5 0.1 convert_bitcast_fusion
  119.6 100.5 %all-gather.12.cloned.1.call-done = bf16[32,172,768]{2,1,0:T(8,128)(2,1)} async-done(((bf16[1,172,768]{2,1,0:T(8,128)(2,1)}), bf16[32,172,768]{2,1,0:T(8,128)(2,1)}) %all-gather.12.cloned.1.call-update) | async-done | bytes 8454160 | tf_op jit(solution)/shard_map/all_gather | solution.py:15
  220.1 12.5 %reshape.30 = bf16[5504,768]{1,0:T(8,128)(2,1)} reshape(bf16[32,172,768]{2,1,0:T(8,128)(2,1)} %all-gather.12.cloned.1.call-done) | data formatting | bytes 16908288
  232.6 5.2 %fusion.2 = bf16[172,768]{1,0:T(8,128)(2,1)S(1)} fusion(bf16[172,5504]{1,0:T(8,128)(2,1)S(1)} %copy-done, bf16[5504,768]{1,0:T(8,128)(2,1)} %reshape.30, f32[768]{0:T(1024)S(1)} %convert_bitcast_fusion), kind=kOutput, calls=%fused_computation.3 | convolution fusion | flops 1454376960 | bytes 10614784 | tf_op jit(solution)/shard_map/dot_general | solution.py:13
  237.7 0.3 reshape.26
  238.0 80.5 %all-gather.8.cloned.1.call-done = bf16[768,4096]{1,0:T(8,128)(2,1)} async-done(((bf16[768,128]{1,0:T(8,128)(2,1)}), bf16[768,4096]{1,0:T(8,128)(2,1)}) %all-gather.8.cloned.1.call-update) | async-done | bytes 6291472 | tf_op jit(solution)/shard_map/all_gather | solution.py:10
  318.6 8.5 %fusion.7 = bf16[6,172,4096]{2,1,0:T(8,128)(2,1)} fusion(bf16[6,128,4096]{2,1,0:T(8,128)(2,1)} %bitcast.14, bf16[172,6,128]{2,1,0:T(8,128)(2,1)S(1)} %reshape.26), kind=kOutput, calls=%fused_computation.8 | convolution fusion | flops 1082130432 | bytes 15009792 | tf_op jit(solution)/shard_map/jst,std->sjd/dot_general | solution.py:24
  327.1 51.2 %all-gather.10.cloned.1.call-done = bf16[4,172,4096]{2,0,1:T(4,128)(2,1)} async-done(((bf16[4,172,256]{2,0,1:T(4,128)(2,1)}), bf16[4,172,4096]{2,0,1:T(4,128)(2,1)}) %all-gather.10.cloned.1.call-update) | async-done | bytes 5636112 | tf_op jit(solution)/shard_map/all_gather | solution.py:33
  378.3 15.5 %fusion.3 = f32[6,4]{0,1:T(4,128)S(1)} fusion(bf16[4,172,4096]{2,0,1:T(4,128)(2,1)} %all-gather.10.cloned.1.call-done, bf16[6,172,4096]{2,1,0:T(8,128)(2,1)} %fusion.7), kind=kOutput, calls=%fused_computation.5 | convolution fusion | flops 33816576 | bytes 14090336 | tf_op jit(solution)/shard_map/sij,qij->sq/dot_general | solution.py:30
  393.8 73.8 %psum.7 = f32[6,4]{0,1:T(4,128)S(1)} all-reduce(f32[6,4]{0,1:T(4,128)S(1)} %fusion.3), channel_id=1, replica_groups=mesh['dp'=16,'tensor'=32] {'tensor'}, use_global_device_ids=true, to_apply=%region_0.0 | all-reduce | flops 24 | bytes 192 | tf_op jit(solution)/shard_map/psum | solution.py:35
  467.6 0.6 broadcast_multiply_fusion
  (7 shorter events, 0.0 us)
Async XLA Ops:
  6.5 226.0 %copy-start = (bf16[172,5504]{1,0:T(8,128)(2,1)S(1)}, bf16[172,5504]{1,0:T(8,128)(2,1)}, u32[]{:S(2)}) copy-start(bf16[172,5504]{1,0:T(8,128)(2,1)} %param.11) | copy-start | bytes 5680132
  6.5 111.9 %copy-start.2 = (f32[172,256]{1,0:T(8,128)S(1)}, f32[172,256]{1,0:T(8,128)}, u32[]{:S(2)}) copy-start(f32[172,256]{1,0:T(8,128)} %param.13) | copy-start | bytes 528388
  6.5 112.0 %copy-start.1 = (bf16[4,172,256]{2,0,1:T(4,128)(2,1)S(1)}, bf16[4,172,256]{2,0,1:T(4,128)(2,1)}, u32[]{:S(2)}) copy-start(bf16[4,172,256]{2,0,1:T(4,128)(2,1)} %param.12) | copy-start | bytes 1056772
  6.5 112.9 %copy-start.3 = (s32[6]{0:T(128)S(1)}, s32[6]{0:T(128)}, u32[]{:S(2)}) copy-start(s32[6]{0:T(128)} %param.15) | copy-start | bytes 76
  6.5 105.7 %all-gather.6.cloned.1.call-start = ((), (), s32[]{:S(2)}) async-start(), calls=%async_computation | async-start | bytes 6488064 | tf_op jit(solution)/shard_map/all_gather | solution.py:8
  7.3 212.8 %all-gather.12.cloned.1.call-start = ((), (), s32[]{:S(2)}) async-start(), calls=%async_computation.3 | async-start | bytes 8921088 | tf_op jit(solution)/shard_map/all_gather | solution.py:15
  8.0 310.6 %all-gather.8.cloned.1.call-start = ((), (), s32[]{:S(2)}) async-start(), calls=%async_computation.1 | async-start | bytes 6488064 | tf_op jit(solution)/shard_map/all_gather | solution.py:10
  117.8 260.5 %all-gather.10.cloned.1.call-start = ((), (), s32[]{:S(2)}) async-start(), calls=%async_computation.2 | async-start | bytes 5988352 | tf_op jit(solution)/shard_map/all_gather | solution.py:33
Sparse Core Ops, SparseCore 0:
  10.4 101.8 all-gather.5
  115.4 104.6 all-gather.11
  223.1 95.4 all-gather.7
  320.5 57.7 all-gather.9
where the time goes:
time: 475 us
  waiting for transfers between devices  338 us (71%)
  blocking collectives  73.8 us (16%)
  matrix products  34.7 us (7%)
  between operations  13.8 us (3%)
  local copies, waits for them, and re-layouts  12.8 us (3%)
    all_gather x1, waiting for transfers between devices, local(): full_act = lax.all_gather(activations, 'tensor', axis=1, tiled=True)  104 us
    all_gather x1, waiting for transfers between devices, local(): lax.all_gather(out_grads_t, 'tensor', axis=0, tiled=True)  101 us
    all_gather x1, waiting for transfers between devices, local(): act_proj = lax.all_gather(act_local, 'tensor', axis=1, tiled=True)  80.5 us
    psum x1, blocking collectives, local(): totals = lax.psum(partial_value, 'tensor')  73.8 us
    all_gather x1, waiting for transfers between devices, local(): lax.all_gather(scaled, 'dp', axis=2, tiled=True).astype(jnp.float32)  51.2 us
    dot_general x1, matrix products, local(): jnp.einsum('sij,qij->sq', projected, lax.all_gather(scaled, 'dp', axis=2,...  15.5 us
    unnamed x9, local copies, waits for them, and re-layouts  12.5 us
  transfers between devices with their start and end apart: 4, of which 4 were waited for; matrix products, arithmetic and copies ran while one was open for 7% of the time, Pallas kernels for 0%

commit v1 on v0

--- a/solution.py
+++ b/solution.py
@@ -2,6 +2,31 @@
 import jax.numpy as jnp
 from jax import lax
 from jax.sharding import PartitionSpec as P
+
+
+def _load_islands(page, in_dim):
+    heard = lax.axis_size("dp")
+    now, all_rows, next_value = (heard, lax.axis_index("dp"), page.shape[in_dim])
+    buffers = [it * now if k0 == in_dim else it for k0, it in enumerate(page.shape)]
+    later = kept_arr = page
+    piece_next = lax.dynamic_update_slice_in_dim(
+        jnp.zeros(buffers, page.dtype), page, all_rows * next_value, axis=in_dim
+    )
+    for dev_i in range(1, now // 2 + 1):
+        later = lax.ppermute(
+            later, axis_name="dp", perm=list(map(lambda k0: (k0, (k0 + 1) % now), range(now)))
+        )
+        piece_next = lax.dynamic_update_slice_in_dim(
+            piece_next, later, (all_rows - dev_i) % now * next_value, axis=in_dim
+        )
+        if 2 * dev_i < now:
+            kept_arr = lax.ppermute(
+                kept_arr, "dp", perm=list(map(lambda k0: (k0, (k0 - 1) % now), range(now)))
+            )
+            piece_next = lax.dynamic_update_slice_in_dim(
+                piece_next, kept_arr, (all_rows + dev_i) % now * next_value, axis=in_dim
+            )
+    return piece_next
 
 
 def local(activations, out_grads_t, in_basis, out_basis_t, query_proj, eigvals, damping, lengths):
@@ -28,9 +53,7 @@
         preferred_element_type=jnp.float32,
     )
     partial_value = jnp.einsum(
-        "sij,qij->sq",
-        projected,
-        lax.all_gather(scaled, "dp", axis=2, tiled=True).astype(jnp.float32),
+        "sij,qij->sq", projected, _load_islands(scaled, 2).astype(jnp.float32)
     )
     totals = lax.psum(partial_value, "tensor")
     norm_factor = (act_proj.shape[1] * out_basis_t.shape[1] * seq_len) ** (-0.5)

time: 475 us -> 425 us (0.89)
  waiting for transfers between devices: 338 us -> 251 us
  local copies, waits for them, and re-layouts: 12.8 us -> 34.5 us
  starting transfers between devices: 0.15 us -> 13.4 us
    all_gather x1, waiting for transfers between devices: 101 us -> 37.5 us  [local(): lax.all_gather(out_grads_t, 'tensor', axis=0, tiled=True)]
    all_gather x1 -> x0, waiting for transfers between devices: 51.2 us -> none  [local(): lax.all_gather(scaled, 'dp', axis=2, tiled=True).astype(jnp.float32)]
    ppermute x0 -> x15, waiting for transfers between devices: none -> 27.7 us  [the longest x8 26.2 us: _load_islands(): lax.ppermute(later, axis_name='dp', perm=list(map(lambda k0: (k0, (k0 + 1...]
    dynamic_update_slice x0 -> x15, local copies, waits for them, and re-layouts: none -> 16.4 us  [the longest x7 8.3 us: _load_islands(): lax.dynamic_update_slice_in_dim(piece_next, kept_arr, (all_rows + dev_i)...]
    ppermute x0 -> x15, starting transfers between devices: none -> 13.4 us  [the longest x7 13.3 us: _load_islands(): lax.ppermute(kept_arr, 'dp', perm=list(map(lambda k0: (k0, (k0 - 1) % now...]
    broadcast_in_dim x0 -> x1, local copies, waits for them, and re-layouts: none -> 5.22 us  [_load_islands(): jnp.zeros(buffers, page.dtype)]
    unnamed x9 -> x13, local copies, waits for them, and re-layouts: 12.5 us -> 12.5 us
  transfers between devices with their start and end apart: 4 -> 18, of which waited for: 4 -> 13; matrix products, arithmetic and copies ran while one was open for 7% -> 11% of each run, Pallas kernels for 0% -> 0%
where the time goes in v1:
time: 425 us; the launch traced here: 424 us
  waiting for transfers between devices  251 us (59%)
  blocking collectives  74.5 us (18%)
  matrix products  34.7 us (8%)
  local copies, waits for them, and re-layouts  34.5 us (8%)
  between operations  14.1 us (3%)
  starting transfers between devices  13.4 us (3%)
    all_gather x1, waiting for transfers between devices, local(): full_act = lax.all_gather(activations, 'tensor', axis=1, tiled=True)  104 us
    all_gather x1, waiting for transfers between devices, local(): act_proj = lax.all_gather(act_local, 'tensor', axis=1, tiled=True)  80.5 us
    psum x1, blocking collectives, local(): totals = lax.psum(partial_value, 'tensor')  74.5 us
    all_gather x1, waiting for transfers between devices, local(): lax.all_gather(out_grads_t, 'tensor', axis=0, tiled=True)  37.5 us
    ppermute x8, waiting for transfers between devices, _load_islands(): lax.ppermute(later, axis_name='dp', perm=list(map(lambda k0: (k0, (k0 + 1...  26.2 us
    dot_general x1, matrix products, local(): jnp.einsum('sij,qij->sq', projected, _load_islands(scaled, 2).astype(jnp....  15.5 us
    ppermute x7, starting transfers between devices, _load_islands(): lax.ppermute(kept_arr, 'dp', perm=list(map(lambda k0: (k0, (k0 - 1) % now...  13.3 us
    unnamed x13, local copies, waits for them, and re-layouts  12.5 us
  transfers between devices with their start and end apart: 18, of which 13 were waited for; matrix products, arithmetic and copies ran while one was open for 11% of the time, Pallas kernels for 0%

profile of v1, /device:TPU:64, one launch (start us, length us, event | category | flops | bytes accessed | tf_op | source)
XLA Modules:
  0.0 424.2 jit_solution(1566481740816497662)
XLA Ops:
  8.1 104.2 %all-gather.5.cloned.1.call-done = bf16[768,4096]{1,0:T(8,128)(2,1)} async-done(((bf16[768,128]{1,0:T(8,128)(2,1)}), bf16[768,4096]{1,0:T(8,128)(2,1)}) %all-gather.5.cloned.1.call-update) | async-done | bytes 6291472 | tf_op jit(solution)/shard_map/all_gather | solution.py:33
  112.3 5.5 %convolution_convert_fusion = bf16[768,128]{1,0:T(8,128)(2,1)} fusion(bf16[768,4096]{1,0:T(8,128)(2,1)} %all-gather.5.cloned.1.call-done, bf16[4096,128]{1,0:T(8,128)(2,1)} %param.10), kind=kOutput, calls=%fused_computation.4 | convolution fusion | flops 805404672 | bytes 7536640 | tf_op jit(solution)/shard_map/dot_general | solution.py:34
  118.5 5.2 %broadcast_in_dim.2 = bf16[4,172,4096]{2,0,1:T(4,128)(2,1)} broadcast(bf16[]{:T(256)} %constant.91.clone.1), dimensions={} | broadcast | bytes 5636098 | tf_op jit(solution)/shard_map/broadcast_in_dim | solution.py:13
  124.7 1.7 collective-permute-start.1
  126.5 5.0 %collective-permute-done = bf16[4,172,256]{2,0,1:T(4,128)(2,1)S(1)} collective-permute-done((bf16[4,172,256]{2,0,1:T(4,128)(2,1)S(1)}, bf16[4,172,256]{2,0,1:T(4,128)(2,1)S(1)}, u32[]{:S(2)}, u32[]{:S(2)}) %collective-permute-start) | collective-permute-done | bytes 352288 | tf_op jit(solution)/shard_map/ppermute | solution.py:16
  131.5 1.7 collective-permute-start.3
  133.2 5.0 %collective-permute-done.2 = bf16[4,172,256]{2,0,1:T(4,128)(2,1)S(1)} collective-permute-done((bf16[4,172,256]{2,0,1:T(4,128)(2,1)S(1)}, bf16[4,172,256]{2,0,1:T(4,128)(2,1)S(1)}, u32[]{:S(2)}, u32[]{:S(2)}) %collective-permute-start.2) | collective-permute-done | bytes 352288 | tf_op jit(solution)/shard_map/ppermute | solution.py:16
  138.3 2.1 collective-permute-start.5
  140.4 4.6 %collective-permute-done.4 = bf16[4,172,256]{2,0,1:T(4,128)(2,1)S(1)} collective-permute-done((bf16[4,172,256]{2,0,1:T(4,128)(2,1)S(1)}, bf16[4,172,256]{2,0,1:T(4,128)(2,1)S(1)}, u32[]{:S(2)}, u32[]{:S(2)}) %collective-permute-start.4) | collective-permute-done | bytes 352288 | tf_op jit(solution)/shard_map/ppermute | solution.py:16
  145.3 1.9 constant_dynamic-update-slice_fusion.14
  148.7 1.9 constant_dynamic-update-slice_fusion.13
  152.7 1.9 constant_dynamic-update-slice_fusion.11
  154.5 1.8 collective-permute-start.9
  161.2 2.2 collective-permute-start.11
  168.2 2.2 collective-permute-start.13
  171.3 2.3 collective-permute-done.12
  176.3 5.2 %collective-permute-done.14 = bf16[4,172,256]{2,0,1:T(4,128)(2,1)S(1)} collective-permute-done((bf16[4,172,256]{2,0,1:T(4,128)(2,1)S(1)}, bf16[4,172,256]{2,0,1:T(4,128)(2,1)S(1)}, u32[]{:S(2)}, u32[]{:S(2)}) %collective-permute-start.14) | collective-permute-done | bytes 352288 | tf_op jit(solution)/shard_map/ppermute | solution.py:16
  182.5 37.5 %all-gather.9.cloned.1.call-done = bf16[32,172,768]{2,1,0:T(8,128)(2,1)} async-done(((bf16[1,172,768]{2,1,0:T(8,128)(2,1)}), bf16[32,172,768]{2,1,0:T(8,128)(2,1)}) %all-gather.9.cloned.1.call-update) | async-done | bytes 8454160 | tf_op jit(solution)/shard_map/all_gather | solution.py:40
  220.0 12.5 %reshape.30 = bf16[5504,768]{1,0:T(8,128)(2,1)} reshape(bf16[32,172,768]{2,1,0:T(8,128)(2,1)} %all-gather.9.cloned.1.call-done) | data formatting | bytes 16908288
  232.5 5.2 %fusion.2 = bf16[172,768]{1,0:T(8,128)(2,1)S(1)} fusion(bf16[172,5504]{1,0:T(8,128)(2,1)S(1)} %copy-done, bf16[5504,768]{1,0:T(8,128)(2,1)} %reshape.30, f32[768]{0:T(1024)S(1)} %convert_bitcast_fusion), kind=kOutput, calls=%fused_computation.3 | convolution fusion | flops 1454376960 | bytes 10614784 | tf_op jit(solution)/shard_map/dot_general | solution.py:38
  238.0 80.5 %all-gather.7.cloned.1.call-done = bf16[768,4096]{1,0:T(8,128)(2,1)} async-done(((bf16[768,128]{1,0:T(8,128)(2,1)}), bf16[768,4096]{1,0:T(8,128)(2,1)}) %all-gather.7.cloned.1.call-update) | async-done | bytes 6291472 | tf_op jit(solution)/shard_map/all_gather | solution.py:35
  318.5 8.5 %fusion.7 = bf16[6,172,4096]{2,1,0:T(8,128)(2,1)} fusion(bf16[6,128,4096]{2,1,0:T(8,128)(2,1)} %bitcast.14, bf16[172,6,128]{2,1,0:T(8,128)(2,1)S(1)} %reshape.26), kind=kOutput, calls=%fused_computation.8 | convolution fusion | flops 1082130432 | bytes 15009792 | tf_op jit(solution)/shard_map/jst,std->sjd/dot_general | solution.py:49
  327.0 15.5 %fusion.3 = f32[6,4]{0,1:T(4,128)S(1)} fusion(bf16[4,172,4096]{2,0,1:T(4,128)(2,1)} %constant_dynamic-update-slice_fusion, bf16[6,172,4096]{2,1,0:T(8,128)(2,1)} %fusion.7), kind=kOutput, calls=%fused_computation.5 | convolution fusion | flops 33816576 | bytes 14090336 | tf_op jit(solution)/shard_map/sij,qij->sq/dot_general | solution.py:55
  342.6 74.5 %psum.7 = f32[6,4]{0,1:T(4,128)S(1)} all-reduce(f32[6,4]{0,1:T(4,128)S(1)} %fusion.3), channel_id=1, replica_groups=mesh['dp'=16,'tensor'=32] {'tensor'}, use_global_device_ids=true, to_apply=%region_0.1 | all-reduce | flops 24 | bytes 192 | tf_op jit(solution)/shard_map/psum | solution.py:58
  (54 shorter events, 21.4 us)
Async XLA Ops:
  6.5 225.9 %copy-start = (bf16[172,5504]{1,0:T(8,128)(2,1)S(1)}, bf16[172,5504]{1,0:T(8,128)(2,1)}, u32[]{:S(2)}) copy-start(bf16[172,5504]{1,0:T(8,128)(2,1)} %param.11) | copy-start | bytes 5680132
  6.5 111.9 %copy-start.4 = (f32[172,256]{1,0:T(8,128)S(1)}, f32[172,256]{1,0:T(8,128)}, u32[]{:S(2)}) copy-start(f32[172,256]{1,0:T(8,128)} %param.13) | copy-start | bytes 528388
  6.5 105.7 %all-gather.5.cloned.1.call-start = ((), (), s32[]{:S(2)}) async-start(), calls=%async_computation | async-start | bytes 6488064 | tf_op jit(solution)/shard_map/all_gather | solution.py:33
  7.3 212.7 %all-gather.9.cloned.1.call-start = ((), (), s32[]{:S(2)}) async-start(), calls=%async_computation.2 | async-start | bytes 8921088 | tf_op jit(solution)/shard_map/all_gather | solution.py:40
  8.0 115.7 %copy-start.3 = (bf16[4,172,256]{2,0,1:T(4,128)(2,1)S(1)}, bf16[4,172,256]{2,0,1:T(4,128)(2,1)}, u32[]{:S(2)}) copy-start(bf16[4,172,256]{2,0,1:T(4,128)(2,1)} %param.12) | copy-start | bytes 1056772
  8.0 310.5 %all-gather.7.cloned.1.call-start = ((), (), s32[]{:S(2)}) async-start(), calls=%async_computation.1 | async-start | bytes 6488064 | tf_op jit(solution)/shard_map/all_gather | solution.py:35
  117.8 27.3 %copy-start.5 = (s32[6]{0:T(128)S(1)}, s32[6]{0:T(128)}, u32[]{:S(2)}) copy-start(s32[6]{0:T(128)} %param.15) | copy-start | bytes 76
  124.7 6.8 %collective-permute-start = (bf16[4,172,256]{2,0,1:T(4,128)(2,1)S(1)}, bf16[4,172,256]{2,0,1:T(4,128)(2,1)S(1)}, u32[]{:S(2)}, u32[]{:S(2)}) collective-permute-start(bf16[4,172,256]{2,0,1:T(4,128)(2,1)S(1)} %get-tuple-element.6), channel_id=1, source_target_pairs={{0,32},{32,64},{64,96},{96,128},{128,160},{160,192},{192,224},{224... | collective-permute-start | bytes 1056776 | tf_op jit(solution)/shard_map/ppermute | solution.py:16
  124.7 6.8 %collective-permute-start.1 = (bf16[4,172,256]{2,0,1:T(4,128)(2,1)S(1)}, bf16[4,172,256]{2,0,1:T(4,128)(2,1)S(1)}, u32[]{:S(2)}, u32[]{:S(2)}) collective-permute-start(bf16[4,172,256]{2,0,1:T(4,128)(2,1)S(1)} %get-tuple-element.6), channel_id=1, source_target_pairs={{0,480},{32,0},{64,32},{96,64},{128,96},{160,128},{192,160},{224,1... | collective-permute-start | bytes 1056776 | tf_op jit(solution)/shard_map/ppermute | solution.py:23
  131.5 8.9 %copy-start.2 = (bf16[4,172,256]{2,0,1:T(4,128)(2,1)}, bf16[4,172,256]{2,0,1:T(4,128)(2,1)S(1)}, u32[]{:S(2)}) copy-start(bf16[4,172,256]{2,0,1:T(4,128)(2,1)S(1)} %collective-permute-done) | copy-start | bytes 1056772
  131.5 6.8 %collective-permute-start.2 = (bf16[4,172,256]{2,0,1:T(4,128)(2,1)S(1)}, bf16[4,172,256]{2,0,1:T(4,128)(2,1)S(1)}, u32[]{:S(2)}, u32[]{:S(2)}) collective-permute-start(bf16[4,172,256]{2,0,1:T(4,128)(2,1)S(1)} %collective-permute-done), channel_id=1, source_target_pairs={{0,32},{32,64},{64,96},{96,128},{128,160},{160,192},{192,224},{224... | collective-permute-start | bytes 1056776 | tf_op jit(solution)/shard_map/ppermute | solution.py:16
  131.5 6.8 %copy-start.1 = (bf16[4,172,256]{2,0,1:T(4,128)(2,1)}, bf16[4,172,256]{2,0,1:T(4,128)(2,1)S(1)}, u32[]{:S(2)}) copy-start(bf16[4,172,256]{2,0,1:T(4,128)(2,1)S(1)} %collective-permute-done.1) | copy-start | bytes 1056772
  131.5 6.8 %collective-permute-start.3 = (bf16[4,172,256]{2,0,1:T(4,128)(2,1)S(1)}, bf16[4,172,256]{2,0,1:T(4,128)(2,1)}, u32[]{:S(2)}, u32[]{:S(2)}) collective-permute-start(bf16[4,172,256]{2,0,1:T(4,128)(2,1)S(1)} %collective-permute-done.1), channel_id=1, source_target_pairs={{0,480},{32,0},{64,32},{96,64},{128,96},{160,128},{192,160},{224,1... | collective-permute-start | bytes 1056776 | tf_op jit(solution)/shard_map/ppermute | solution.py:23
  138.2 6.8 %collective-permute-start.4 = (bf16[4,172,256]{2,0,1:T(4,128)(2,1)S(1)}, bf16[4,172,256]{2,0,1:T(4,128)(2,1)S(1)}, u32[]{:S(2)}, u32[]{:S(2)}) collective-permute-start(bf16[4,172,256]{2,0,1:T(4,128)(2,1)S(1)} %collective-permute-done.2), channel_id=1, source_target_pairs={{0,32},{32,64},{64,96},{96,128},{128,160},{160,192},{192,224},{224... | collective-permute-start | bytes 1056776 | tf_op jit(solution)/shard_map/ppermute | solution.py:16
  138.3 8.9 %collective-permute-start.5 = (bf16[4,172,256]{2,0,1:T(4,128)(2,1)}, bf16[4,172,256]{2,0,1:T(4,128)(2,1)S(1)}, u32[]{:S(2)}, u32[]{:S(2)}) collective-permute-start(bf16[4,172,256]{2,0,1:T(4,128)(2,1)} %collective-permute-done.3), channel_id=1, source_target_pairs={{0,480},{32,0},{64,32},{96,64},{128,96},{160,128},{192,160},{224,1... | collective-permute-start | bytes 1056776 | tf_op jit(solution)/shard_map/ppermute | solution.py:23
  145.0 6.8 %collective-permute-start.6 = (bf16[4,172,256]{2,0,1:T(4,128)(2,1)S(1)}, bf16[4,172,256]{2,0,1:T(4,128)(2,1)S(1)}, u32[]{:S(2)}, u32[]{:S(2)}) collective-permute-start(bf16[4,172,256]{2,0,1:T(4,128)(2,1)S(1)} %collective-permute-done.4), channel_id=1, source_target_pairs={{0,32},{32,64},{64,96},{96,128},{128,160},{160,192},{192,224},{224... | collective-permute-start | bytes 1056776 | tf_op jit(solution)/shard_map/ppermute | solution.py:16
  147.2 7.4 %collective-permute-start.7 = (bf16[4,172,256]{2,0,1:T(4,128)(2,1)S(1)}, bf16[4,172,256]{2,0,1:T(4,128)(2,1)S(1)}, u32[]{:S(2)}, u32[]{:S(2)}) collective-permute-start(bf16[4,172,256]{2,0,1:T(4,128)(2,1)S(1)} %collective-permute-done.5), channel_id=1, source_target_pairs={{0,480},{32,0},{64,32},{96,64},{128,96},{160,128},{192,160},{224,1... | collective-permute-start | bytes 1056776 | tf_op jit(solution)/shard_map/ppermute | solution.py:23
  151.8 6.8 %collective-permute-start.8 = (bf16[4,172,256]{2,0,1:T(4,128)(2,1)S(1)}, bf16[4,172,256]{2,0,1:T(4,128)(2,1)S(1)}, u32[]{:S(2)}, u32[]{:S(2)}) collective-permute-start(bf16[4,172,256]{2,0,1:T(4,128)(2,1)S(1)} %collective-permute-done.6), channel_id=1, source_target_pairs={{0,32},{32,64},{64,96},{96,128},{128,160},{160,192},{192,224},{224... | collective-permute-start | bytes 1056776 | tf_op jit(solution)/shard_map/ppermute | solution.py:16
  154.5 6.6 %collective-permute-start.9 = (bf16[4,172,256]{2,0,1:T(4,128)(2,1)S(1)}, bf16[4,172,256]{2,0,1:T(4,128)(2,1)S(1)}, u32[]{:S(2)}, u32[]{:S(2)}) collective-permute-start(bf16[4,172,256]{2,0,1:T(4,128)(2,1)S(1)} %collective-permute-done.7), channel_id=1, source_target_pairs={{0,480},{32,0},{64,32},{96,64},{128,96},{160,128},{192,160},{224,1... | collective-permute-start | bytes 1056776 | tf_op jit(solution)/shard_map/ppermute | solution.py:23
  158.5 7.3 %collective-permute-start.10 = (bf16[4,172,256]{2,0,1:T(4,128)(2,1)S(1)}, bf16[4,172,256]{2,0,1:T(4,128)(2,1)S(1)}, u32[]{:S(2)}, u32[]{:S(2)}) collective-permute-start(bf16[4,172,256]{2,0,1:T(4,128)(2,1)S(1)} %collective-permute-done.8), channel_id=1, source_target_pairs={{0,32},{32,64},{64,96},{96,128},{128,160},{160,192},{192,224},{224... | collective-permute-start | bytes 1056776 | tf_op jit(solution)/shard_map/ppermute | solution.py:16
  161.2 7.1 %collective-permute-start.11 = (bf16[4,172,256]{2,0,1:T(4,128)(2,1)S(1)}, bf16[4,172,256]{2,0,1:T(4,128)(2,1)S(1)}, u32[]{:S(2)}, u32[]{:S(2)}) collective-permute-start(bf16[4,172,256]{2,0,1:T(4,128)(2,1)S(1)} %collective-permute-done.9), channel_id=1, source_target_pairs={{0,480},{32,0},{64,32},{96,64},{128,96},{160,128},{192,160},{224,1... | collective-permute-start | bytes 1056776 | tf_op jit(solution)/shard_map/ppermute | solution.py:23
  165.8 7.8 %collective-permute-start.12 = (bf16[4,172,256]{2,0,1:T(4,128)(2,1)S(1)}, bf16[4,172,256]{2,0,1:T(4,128)(2,1)S(1)}, u32[]{:S(2)}, u32[]{:S(2)}) collective-permute-start(bf16[4,172,256]{2,0,1:T(4,128)(2,1)S(1)} %collective-permute-done.10), channel_id=1, source_target_pairs={{0,32},{32,64},{64,96},{96,128},{128,160},{160,192},{192,224},{224... | collective-permute-start | bytes 1056776 | tf_op jit(solution)/shard_map/ppermute | solution.py:16
  168.2 7.2 %collective-permute-start.13 = (bf16[4,172,256]{2,0,1:T(4,128)(2,1)S(1)}, bf16[4,172,256]{2,0,1:T(4,128)(2,1)S(1)}, u32[]{:S(2)}, u32[]{:S(2)}) collective-permute-start(bf16[4,172,256]{2,0,1:T(4,128)(2,1)S(1)} %collective-permute-done.11), channel_id=1, source_target_pairs={{0,480},{32,0},{64,32},{96,64},{128,96},{160,128},{192,160},{224,1... | collective-permute-start | bytes 1056776 | tf_op jit(solution)/shard_map/ppermute | solution.py:23
  173.6 8.0 %collective-permute-start.14 = (bf16[4,172,256]{2,0,1:T(4,128)(2,1)S(1)}, bf16[4,172,256]{2,0,1:T(4,128)(2,1)S(1)}, u32[]{:S(2)}, u32[]{:S(2)}) collective-permute-start(bf16[4,172,256]{2,0,1:T(4,128)(2,1)S(1)} %collective-permute-done.12), channel_id=1, source_target_pairs={{0,32},{32,64},{64,96},{96,128},{128,160},{160,192},{192,224},{224... | collective-permute-start | bytes 1056776 | tf_op jit(solution)/shard_map/ppermute | solution.py:16
Sparse Core Ops, SparseCore 0:
  10.4 101.8 all-gather.4
  115.4 104.5 all-gather.8
  223.0 95.4 all-gather.6
